TPU v7x, 128 devices: a whole 4x4x4 slice. The times are simulated.
128 devices in a mesh: gz: 32 (over x, y, core), gy: 4 (over z).
Axes of the slice: x: 4, y: 4, z: 4, core: 2. Of those that a mesh axis runs over, the one named last changes fastest.
Arguments:
- distribution_functions: float32 [19, 128, 36864], P(None, 'gz', 'gy')
- site_phase_kinds: int32 [128, 36864], P('gz', 'gy'), may hold values from 0 to 2
- thermal_state_values: float32 [128, 36864], P('gz', 'gy'), may hold values from 0.5 to 3
- boundary_tile_lines: int32 [128, 64], P(('gz', 'gy')), may hold values from 0 to 287
- wanted_tile_position: int32 [128, 128, 4], P(('gz', 'gy')), may hold values from 0 to 63
- trajectory_hit_places: int32 [128, 512], P(('gz', 'gy')), may hold values from 0 to 511, each once within a row
- hits_along_each_shot: int32 [128, 64], P(('gz', 'gy')), may hold values from 1 to 8
- incident_light_strength: float32 [128, 64, 128], P(('gz', 'gy')), may hold values from 0.5 to 2
Outputs:
- lattice_out: float32 [19, 128, 36864], P(None, 'gz', 'gy')
- temperature_out: float32 [128, 36864], P('gz', 'gy')
Inputs may be any that keep to these rules, and one draw needn't show every extreme that they name: `trajectory_hit_places`: each device's row lists every slot exactly once.
All inputs are finite; a program needn't handle non-finite values.
Results may differ from a plain program's by a relative error of at most 0.0003.
Values sent between devices are 32-bit elements; how exact they have to be, the bound alone decides.
A program may use at most 320 MiB of HBM per device.

v0:
```python
import jax
import jax.numpy as jnp
from jax import lax
from jax.experimental import pallas as pl
from jax.experimental.pallas import tpu as pltpu
from jax.sharding import PartitionSpec as P

MESH = pl.DeviceIdType.MESH
N_GZ = 32
N_GY = 4
DEVICES = 128
CAP = 4
SLOTS = 512
NB_DEV = 64
RAYS = 64
BOUNCES = 8
ACROSS = 192
DEPTH = 4
ROWS = 72
CELL_ROWS = 288
PAD = 8
PLANE = ROWS + 2 * PAD

DIRS = [
    (0, 0, 0),
    (1, 0, 0),
    (-1, 0, 0),
    (0, 1, 0),
    (0, -1, 0),
    (0, 0, 1),
    (0, 0, -1),
    (1, 1, 0),
    (-1, -1, 0),
    (1, -1, 0),
    (-1, 1, 0),
    (1, 0, 1),
    (-1, 0, -1),
    (1, 0, -1),
    (-1, 0, 1),
    (0, 1, 1),
    (0, -1, -1),
    (0, 1, -1),
    (0, -1, 1),
]
WEIGHTS = [1.0 / 3.0] + [1.0 / 18.0] * 6 + [1.0 / 36.0] * 12
PAIRS = [(q, q + 1) for q in range(1, 19, 2)]
OPP = [0, 2, 1, 4, 3, 6, 5, 8, 7, 10, 9, 12, 11, 14, 13, 16, 15, 18, 17]
RELAX = 0.8
ORDER = [18, 5, 11, 14, 15, 17, 12, 13, 6, 16, 4, 8, 9, 1, 2, 0, 3, 7, 10]
SLOT = [ORDER.index(q) for q in range(19)]
LEFT_BIT = 19
RIGHT_BIT = 20


def tile_iota(axis, shape=(8, 128)):
    return lax.broadcasted_iota(jnp.int32, shape, axis)


def moments(f):
    d = {a: f[a] - f[b] for a, b in PAIRS}
    s = {a: f[a] + f[b] for a, b in PAIRS}
    density = (
        ((s[1] + s[3]) + (s[5] + s[7])) + ((s[9] + s[11]) + (s[13] + s[15])) + (s[17] + f[0])
    )
    mx = (d[1] + d[7]) + (d[9] + d[11]) + d[13]
    my = (d[3] + d[7]) + (d[15] - d[9]) + d[17]
    mz = (d[5] + d[11]) + (d[15] - d[13]) - d[17]
    inv = 1.0 / density
    return density, mx * inv, my * inv, mz * inv


def along(u, q):
    total = None
    for step, part in zip(DIRS[q], u):
        if step == 0:
            continue
        if total is None:
            total = part if step > 0 else -part
        else:
            total = total + part if step > 0 else total - part
    return total


def collide(f, gas):
    density, ux, uy, uz = moments(f)
    base = 1.0 - 1.5 * (ux * ux + uy * uy + uz * uz)
    triple = (3.0 * ux, 3.0 * uy, 3.0 * uz)
    kept = [None] * 19
    keep = 1.0 - RELAX
    scaled = {w: (RELAX * w) * density for w in (1.0 / 18.0, 1.0 / 36.0)}
    post = keep * f[0] + (RELAX / 3.0) * density * base
    kept[0] = jnp.where(gas, -f[0], post)
    for a, b in PAIRS:
        wd = scaled[WEIGHTS[a]]
        c = along(triple, a)
        even = wd * (base + 0.5 * (c * c))
        odd = wd * c
        kept[a] = jnp.where(gas, -f[b], keep * f[a] + (even + odd))
        kept[b] = jnp.where(gas, -f[a], keep * f[b] + (even - odd))
    zero = jnp.zeros_like(ux)
    velocity = [jnp.where(gas, zero, v) for v in (ux, uy, uz, base)]
    return kept, velocity


def shifted(load, step_x, step_y, left, right):
    lane = tile_iota(1)

    def flat(by):
        rows, lanes = by // 128, by % 128
        if lanes == 0:
            return load(-rows)
        picked = jnp.where(lane >= 128 - lanes, load(-rows - 1), load(-rows))
        return pltpu.roll(picked, lanes, 1)

    main = flat(step_x + ACROSS * step_y)
    if step_x == 0:
        return main
    by = step_x + ACROSS * step_y - ACROSS * step_x
    rows, lanes = by // 128, by % 128
    targets = (0, 64) if step_x == 1 else (63, 127)
    if all(t < lanes for t in targets):
        wrapped = pltpu.roll(load(-rows - 1), lanes, 1)
    elif all(t >= lanes for t in targets):
        wrapped = pltpu.roll(load(-rows), lanes, 1)
    else:
        wrapped = flat(by)
    return jnp.where(left if step_x == 1 else right, wrapped, main)


def window(ref, lead, z, rb):
    def load(n):
        return ref[(*lead, z, pl.ds(rb * 8 + (PAD + n), 8), slice(None))]

    return load


def passed(post_ref, mask_ref, vel_ref, z, rb):
    mask = mask_ref[z, pl.ds(rb * 8, 8), :]
    left = (mask & (1 << LEFT_BIT)) != 0
    right = (mask & (1 << RIGHT_BIT)) != 0
    ux, uy, uz, base = [vel_ref[i, z, pl.ds(rb * 8, 8), :] for i in range(4)]
    centre = [post_ref[SLOT[q], z + 1, pl.ds(rb * 8 + PAD, 8), :] for q in range(19)]
    new = [None] * 19
    new[0] = jnp.where((mask & 1) != 0, -centre[0], centre[0])
    triple = (3.0 * ux, 3.0 * uy, 3.0 * uz)
    for a, b in PAIRS:
        c = along(triple, a)
        both = (2.0 * WEIGHTS[a]) * (base + 0.5 * (c * c))
        for q, back in ((a, b), (b, a)):
            step_x, step_y, step_z = DIRS[q]
            source = shifted(
                window(post_ref, (SLOT[q],), z + 1 - step_z, rb), step_x, step_y, left, right
            )
            new[q] = jnp.where((mask & (1 << q)) != 0, both - centre[back], source)
    return new, (mask & 1) != 0


def two_terms(x):
    high = x.astype(jnp.bfloat16)
    low = (x - high.astype(jnp.float32)).astype(jnp.bfloat16)
    return jnp.concatenate([high, low], axis=1)


def pick(one_hot, values):
    both = jnp.dot(one_hot, two_terms(values), preferred_element_type=jnp.float32)
    return both[:, :128] + both[:, 128:]


def edge_tile(j):
    late = lax.div(j, 18)
    k = j - 18
    z = (1 - late) * (lax.div(j, 9) * 3) + late * (1 + lax.div(k, 2))
    rb = (1 - late) * lax.rem(j, 9) + late * (lax.rem(k, 2) * 8)
    return z, rb


def inner_tile(j):
    return 1 + lax.div(j, 7), 1 + lax.rem(j, 7)


def kernel(
    pop_hbm,
    kind_hbm,
    temp_hbm,
    line_hbm,
    want_hbm,
    place_hbm,
    hits_hbm,
    beam_hbm,
    out_hbm,
    temp_out_hbm,
    field,
    kind,
    temp,
    line,
    want,
    place,
    hits,
    beam,
    gas_pad,
    post1,
    post2,
    mask,
    vel,
    cells,
    ask_send,
    ask_recv,
    row_send,
    row_recv,
    heat_send,
    heat_recv,
    slot_hot,
    ray_hot,
    cell_hot,
    back_hot,
    ray_rows,
    live,
    thermal,
    temp_out,
    load_sem,
    small_sem,
    out_sem,
    gas_s,
    gas_r,
    halo_s,
    halo_r,
    all_s,
    all_r,
    th_s,
    th_r,
    row_sem,
):
    gz = lax.axis_index("gz")
    gy = lax.axis_index("gy")
    me = gz * N_GY + gy
    up, down = lax.rem(gz + 1, N_GZ), lax.rem(gz + N_GZ - 1, N_GZ)
    north, south = lax.rem(gy + 1, N_GY), lax.rem(gy + N_GY - 1, N_GY)

    barrier = pltpu.get_barrier_semaphore()

    def greet(i, carry):
        pl.semaphore_signal(
            barrier, 1, device_id=(lax.rem(gz + i, N_GZ), gy), device_id_type=MESH
        )
        return carry

    lax.fori_loop(1, N_GZ, greet, 0)
    for i in range(1, N_GY):
        pl.semaphore_signal(barrier, 1, device_id=(gz, lax.rem(gy + i, N_GY)), device_id_type=MESH)
    for peer in ((up, north), (up, south), (down, north), (down, south)):
        pl.semaphore_signal(barrier, 1, device_id=peer, device_id_type=MESH)

    small = []
    for i, (src, dst) in enumerate(
        (
            (kind_hbm, kind),
            (want_hbm, want),
            (line_hbm, line),
            (place_hbm, place),
            (hits_hbm, hits),
            (beam_hbm, beam),
            (temp_hbm, temp),
        )
    ):
        copy = pltpu.make_async_copy(src, dst, small_sem.at[i])
        copy.start()
        small.append(copy)

    def part(rb):
        rows = pl.ds(rb * 32, 32)
        return pltpu.make_async_copy(
            pop_hbm.at[:, rows], field.at[:, rows], load_sem.at[rb]
        )

    def start_part(rb, carry):
        part(rb).start()
        return carry

    lax.fori_loop(0, 9, start_part, 0)
    small[0].wait()

    def first(rb, carry):
        part(rb).wait()
        for z in range(DEPTH):
            rows = pl.ds(rb * 32 + z, 8, stride=DEPTH)
            gas = kind[rows, :] == 0
            gas_pad[z + 1, pl.ds(rb * 8 + PAD, 8), :] = gas.astype(jnp.int32)
            kept, velocity = collide([field[q, rows, :] for q in range(19)], gas)
            for q in range(19):
                post1[SLOT[q], z + 1, pl.ds(rb * 8 + PAD, 8), :] = kept[q]
            for i in range(4):
                vel[i, z, pl.ds(rb * 8, 8), :] = velocity[i]
        return carry

    lax.fori_loop(0, 9, first, 0)

    pl.semaphore_wait(barrier, N_GZ - 1 + N_GY - 1 + 4)

    low_src, low_dst = slice(PAD, PAD + 2), slice(PAD + ROWS, PAD + ROWS + 2)
    high_src, high_dst = slice(PAD + ROWS - 2, PAD + ROWS), slice(PAD - 2, PAD)
    body = slice(PAD, PAD + ROWS)
    planes = slice(1, 1 + DEPTH)

    def send(ref, src, dst, s, r, peer):
        copy = pltpu.make_async_remote_copy(
            src_ref=ref.at[src],
            dst_ref=ref.at[dst],
            send_sem=s,
            recv_sem=r,
            device_id=peer,
            device_id_type=MESH,
        )
        copy.start()
        return copy

    def halo(ref, first_sem):
        moves = (
            ((slice(0, 5), 4, body), (slice(0, 5), 0, body), (up, gy)),
            ((slice(5, 10), 1, body), (slice(5, 10), 5, body), (down, gy)),
            ((slice(4, 6), planes, high_src), (slice(4, 6), planes, high_dst), (gz, north)),
            ((slice(16, 19), planes, high_src), (slice(16, 19), planes, high_dst), (gz, north)),
            ((slice(9, 13), planes, low_src), (slice(9, 13), planes, low_dst), (gz, south)),
            ((slice(0, 1), planes, low_src), (slice(0, 1), planes, low_dst), (gz, south)),
            ((4, 4, high_src), (4, 0, high_dst), (up, north)),
            ((9, 1, low_src), (9, 5, low_dst), (down, south)),
            ((5, 1, high_src), (5, 5, high_dst), (down, north)),
            ((0, 4, low_src), (0, 0, low_dst), (up, south)),
        )
        return [
            send(ref, src, dst, halo_s.at[first_sem + i], halo_r.at[first_sem + i], peer)
            for i, (src, dst, peer) in enumerate(moves)
        ]

    gas_moves = (
        ((4, body), (0, body), (up, gy)),
        ((1, body), (5, body), (down, gy)),
        ((planes, high_src), (planes, high_dst), (gz, north)),
        ((planes, low_src), (planes, low_dst), (gz, south)),
        ((4, high_src), (0, high_dst), (up, north)),
        ((4, low_src), (0, low_dst), (up, south)),
        ((1, high_src), (5, high_dst), (down, north)),
        ((1, low_src), (5, low_dst), (down, south)),
    )
    gas_copies = [
        send(gas_pad, src, dst, gas_s.at[i], gas_r.at[i], peer)
        for i, (src, dst, peer) in enumerate(gas_moves)
    ]
    copies1 = halo(post1, 0)

    for i in range(1, N_GY):
        pl.semaphore_signal(row_sem, 1, device_id=(gz, lax.rem(gy + i, N_GY)), device_id_type=MESH)

    for copy in small[1:]:
        copy.wait()
    eye = tile_iota(0, (DEVICES, DEVICES)) == tile_iota(1, (DEVICES, DEVICES))
    lanes = tile_iota(1, (DEVICES, DEVICES))
    rows_of = jnp.zeros((DEVICES, DEVICES), jnp.float32)
    for s in range(CAP):
        asked = want[s : s + 1, :].astype(jnp.float32)
        column = jnp.sum(jnp.where(eye, asked, 0.0), axis=1, keepdims=True)
        rows_of = jnp.where(lanes == s, column, rows_of)
    ask_send[...] = rows_of
    ask_recv[pl.ds(me, 1), :] = ask_send[pl.ds(me, 1), :]
    pl.semaphore_wait(row_sem, N_GY - 1)

    def peer_of(i):
        p = lax.rem(me + i, DEVICES)
        return p, (lax.div(p, N_GY), lax.rem(p, N_GY))

    def ask(i, carry):
        p, peer = peer_of(i)
        pltpu.make_async_remote_copy(
            src_ref=ask_send.at[pl.ds(p, 1)],
            dst_ref=ask_recv.at[pl.ds(me, 1)],
            send_sem=all_s.at[0],
            recv_sem=all_r.at[0],
            device_id=peer,
            device_id_type=MESH,
        ).start()
        return carry

    lax.fori_loop(1, DEVICES, ask, 0)

    for copy in gas_copies:
        copy.wait()

    def masks(j, carry):
        z, rb = lax.div(j, 9), lax.rem(j, 9)
        place_x = lax.rem(
            (rb * 8 + tile_iota(0)) * 128 + tile_iota(1), jnp.full((8, 128), ACROSS, jnp.int32)
        )
        left, right = place_x == 0, place_x == ACROSS - 1
        own = gas_pad[z + 1, pl.ds(rb * 8 + PAD, 8), :]
        bits = own
        for q in range(1, 19):
            step_x, step_y, step_z = DIRS[q]
            source = shifted(window(gas_pad, (), z + 1 - step_z, rb), step_x, step_y, left, right)
            bits = bits | (jnp.maximum(source, own) << q)
        bits = bits | (left.astype(jnp.int32) << LEFT_BIT) | (right.astype(jnp.int32) << RIGHT_BIT)
        mask[z, pl.ds(rb * 8, 8), :] = bits
        return carry

    lax.fori_loop(0, 36, masks, 0)

    def second(tile):
        def step(j, carry):
            z, rb = tile(j)
            new, gas = passed(post1, mask, vel, z, rb)
            kept, velocity = collide(new, gas)
            for q in range(19):
                post2[SLOT[q], z + 1, pl.ds(rb * 8 + PAD, 8), :] = kept[q]
            for i in range(4):
                vel[i, z, pl.ds(rb * 8, 8), :] = velocity[i]
            return carry

        return step

    lax.fori_loop(0, 14, second(inner_tile), 0)
    for copy in copies1:
        copy.wait()
    lax.fori_loop(0, 22, second(edge_tile), 0)
    copies2 = halo(post2, 10)

    big0, big1 = tile_iota(0, (SLOTS, SLOTS)), tile_iota(1, (SLOTS, SLOTS))
    diagonal = big0 == big1
    spot = place[...]
    spot = (spot & 3) * DEVICES + (spot >> 2)
    slot_hot[...] = (big0 == spot).astype(jnp.float32).astype(jnp.bfloat16)
    spot_col = jnp.sum(
        jnp.where(diagonal, spot.astype(jnp.float32), 0.0), axis=1, keepdims=True
    )
    ray_hot[...] = (big1.astype(jnp.float32) == spot_col).astype(jnp.float32).astype(jnp.bfloat16)
    eye_rays = tile_iota(0, (RAYS, RAYS)) == tile_iota(1, (RAYS, RAYS))
    live[...] = jnp.broadcast_to(
        jnp.sum(jnp.where(eye_rays, hits[...].astype(jnp.float32), 0.0), axis=1, keepdims=True),
        (RAYS, 128),
    )
    pltpu.make_async_copy(
        ask_send.at[pl.ds(0, DEVICES - 1)], ask_recv.at[pl.ds(0, DEVICES - 1)], all_r.at[0]
    ).wait()
    block = tile_iota(1, (DEVICES, NB_DEV)).astype(jnp.float32)
    lines = line[...].astype(jnp.float32)
    wanted_row = []
    for s in range(CAP):
        chosen = ask_recv[:, s : s + 1] == block
        wanted_row.append(jnp.sum(jnp.where(chosen, lines, 0.0), axis=1, keepdims=True))
    row_col = jnp.concatenate(wanted_row, axis=0)
    cell_hot[...] = (
        (tile_iota(1, (SLOTS, 384)).astype(jnp.float32) == row_col)
        .astype(jnp.float32)
        .astype(jnp.bfloat16)
    )
    row_row = jnp.sum(jnp.where(diagonal, row_col, 0.0), axis=0, keepdims=True)
    back_hot[...] = (
        (tile_iota(0, (CELL_ROWS, SLOTS)).astype(jnp.float32) == row_row)
        .astype(jnp.float32)
        .astype(jnp.bfloat16)
    )
    cells[CELL_ROWS:, :] = jnp.zeros((384 - CELL_ROWS, 128), jnp.float32)

    def third(tile):
        def step(j, carry):
            z, rb = tile(j)
            new, gas = passed(post2, mask, vel, z, rb)
            rows = pl.ds(rb * 32 + z, 8, stride=DEPTH)
            for q in range(19):
                field[q, rows, :] = new[q]
            density, ux, uy, uz = moments(new)
            for i, v in enumerate((ux, uy, uz)):
                vel[i, z, pl.ds(rb * 8, 8), :] = v
            cosine = 0.2 + 0.7 / (1.0 + jnp.exp(-8.0 * (density - 1.0)))
            index = 1.0 + temp[rows, :]
            upper = (index - cosine) * (index - cosine) + 1.0
            lower = (index + cosine) * (index + cosine) + 1.0
            cells[pl.ds(pl.multiple_of(z * ROWS + rb * 8, 8), 8), :] = jnp.where(
                gas, 1.0, upper / lower
            )
            return carry

        return step

    lax.fori_loop(0, 14, third(inner_tile), 0)
    for copy in copies2:
        copy.wait()
    lax.fori_loop(0, 22, third(edge_tile), 0)
    lattice_copy = pltpu.make_async_copy(field, out_hbm, out_sem.at[0])
    lattice_copy.start()

    def to_all(src, dst, n):
        dst[:, pl.ds(me, 1), :] = src[:, pl.ds(me, 1), :]

        def one(i, carry):
            p, peer = peer_of(i)
            pltpu.make_async_remote_copy(
                src_ref=src.at[:, pl.ds(p, 1)],
                dst_ref=dst.at[:, pl.ds(me, 1)],
                send_sem=all_s.at[n],
                recv_sem=all_r.at[n],
                device_id=peer,
                device_id_type=MESH,
            ).start()
            return carry

        lax.fori_loop(1, DEVICES, one, 0)
        pltpu.make_async_copy(
            src.at[:, pl.ds(0, DEVICES - 1)], dst.at[:, pl.ds(0, DEVICES - 1)], all_r.at[n]
        ).wait()

    row_send[...] = pick(cell_hot[...], cells[...]).reshape(CAP, DEVICES, 128)
    to_all(row_send, row_recv, 1)

    ray_rows[...] = pick(ray_hot[...], row_recv[...].reshape(SLOTS, 128))
    energy = beam[...]
    hit_count = live[...]
    for j in range(BOUNCES):
        at = pl.ds(j, RAYS, stride=BOUNCES)
        ratio = ray_rows[at, :]
        ray_rows[at, :] = jnp.where(hit_count > float(j), energy * (1.0 - ratio), 0.0)
        energy = energy * ratio
    heat_send[...] = pick(slot_hot[...], ray_rows[...]).reshape(CAP, DEVICES, 128)
    to_all(heat_send, heat_recv, 2)

    cells[pl.ds(0, CELL_ROWS), :] = pick(back_hot[...], heat_recv[...].reshape(SLOTS, 128))

    def sources(j, carry):
        z, rb = lax.div(j, 9), lax.rem(j, 9)
        deposit = cells[pl.ds(pl.multiple_of(z * ROWS + rb * 8, 8), 8), :]
        source = temp[pl.ds(rb * 32 + z, 8, stride=DEPTH), :] + deposit
        eighth = 0.125 * source
        for i in range(3):
            moved = eighth * (4.0 * vel[i, z, pl.ds(rb * 8, 8), :])
            thermal[2 * i, z + 1, pl.ds(rb * 8 + PAD, 8), :] = eighth + moved
            thermal[2 * i + 1, z + 1, pl.ds(rb * 8 + PAD, 8), :] = eighth - moved
        cells[pl.ds(pl.multiple_of(z * ROWS + rb * 8, 8), 8), :] = 0.25 * source
        return carry

    lax.fori_loop(0, 36, sources, 0)
    th_moves = (
        ((4, 4, body), (4, 0, body), (up, gy)),
        ((5, 1, body), (5, 5, body), (down, gy)),
        ((2, planes, high_src), (2, planes, high_dst), (gz, north)),
        ((3, planes, low_src), (3, planes, low_dst), (gz, south)),
    )
    th_copies = [
        send(thermal, src, dst, th_s.at[i], th_r.at[i], peer)
        for i, (src, dst, peer) in enumerate(th_moves)
    ]
    for copy in th_copies:
        copy.wait()

    def gather(j, carry):
        z, rb = lax.div(j, 9), lax.rem(j, 9)
        bits = mask[z, pl.ds(rb * 8, 8), :]
        left = (bits & (1 << LEFT_BIT)) != 0
        right = (bits & (1 << RIGHT_BIT)) != 0
        total = cells[pl.ds(pl.multiple_of(z * ROWS + rb * 8, 8), 8), :]
        for i in range(6):
            step_x, step_y, step_z = DIRS[i + 1]
            total = total + shifted(
                window(thermal, (i,), z + 1 - step_z, rb), step_x, step_y, left, right
            )
        temp_out[pl.ds(rb * 32 + z, 8, stride=DEPTH), :] = total
        return carry

    lax.fori_loop(0, 36, gather, 0)
    last = pltpu.make_async_copy(temp_out, temp_out_hbm, out_sem.at[1])
    last.start()
    last.wait()
    lattice_copy.wait()
    pltpu.make_async_copy(
        ask_send.at[pl.ds(0, DEVICES - 1)], ask_recv.at[pl.ds(0, DEVICES - 1)], all_s.at[0]
    ).wait()
    for n, ref in ((1, row_send), (2, heat_send)):
        done = ref.at[:, pl.ds(0, DEVICES - 1)]
        pltpu.make_async_copy(done, done, all_s.at[n]).wait()


def fold(x):
    lead = x.shape[:-2]
    n = len(lead)
    x = x.reshape(lead + (DEPTH, ROWS, 128)).transpose(tuple(range(n)) + (n + 1, n, n + 2))
    return x.reshape(lead + (CELL_ROWS, 128))


def unfold(x):
    lead = x.shape[:-2]
    n = len(lead)
    x = x.reshape(lead + (ROWS, DEPTH, 128)).transpose(tuple(range(n)) + (n + 1, n, n + 2))
    return x.reshape(lead + (DEPTH, ROWS * 128))


def per_device(populations, kinds, temperature, lines, wanted, places, hits, beam):
    f32, i32, bf16 = jnp.float32, jnp.int32, jnp.bfloat16
    dma = pltpu.SemaphoreType.DMA
    lattice, heated = pl.pallas_call(
        kernel,
        out_shape=(
            jax.ShapeDtypeStruct((19, CELL_ROWS, 128), f32),
            jax.ShapeDtypeStruct((CELL_ROWS, 128), f32),
        ),
        in_specs=[pl.BlockSpec(memory_space=pl.ANY)] * 8,
        out_specs=[pl.BlockSpec(memory_space=pl.ANY)] * 2,
        scratch_shapes=[
            pltpu.VMEM((19, CELL_ROWS, 128), f32),
            pltpu.VMEM((CELL_ROWS, 128), i32),
            pltpu.VMEM((CELL_ROWS, 128), f32),
            pltpu.VMEM((1, NB_DEV), i32),
            pltpu.VMEM((CAP, DEVICES), i32),
            pltpu.VMEM((1, SLOTS), i32),
            pltpu.VMEM((1, RAYS), i32),
            pltpu.VMEM((RAYS, 128), f32),
            pltpu.VMEM((DEPTH + 2, PLANE, 128), i32),
            pltpu.VMEM((19, DEPTH + 2, PLANE, 128), f32),
            pltpu.VMEM((19, DEPTH + 2, PLANE, 128), f32),
            pltpu.VMEM((DEPTH, ROWS, 128), i32),
            pltpu.VMEM((4, DEPTH, ROWS, 128), f32),
            pltpu.VMEM((384, 128), f32),
            pltpu.VMEM((DEVICES, 128), f32),
            pltpu.VMEM((DEVICES, 128), f32),
            pltpu.VMEM((CAP, DEVICES, 128), f32),
            pltpu.VMEM((CAP, DEVICES, 128), f32),
            pltpu.VMEM((CAP, DEVICES, 128), f32),
            pltpu.VMEM((CAP, DEVICES, 128), f32),
            pltpu.VMEM((SLOTS, SLOTS), bf16),
            pltpu.VMEM((SLOTS, SLOTS), bf16),
            pltpu.VMEM((SLOTS, 384), bf16),
            pltpu.VMEM((CELL_ROWS, SLOTS), bf16),
            pltpu.VMEM((SLOTS, 128), f32),
            pltpu.VMEM((RAYS, 128), f32),
            pltpu.VMEM((6, DEPTH + 2, PLANE, 128), f32),
            pltpu.VMEM((CELL_ROWS, 128), f32),
            dma((9,)),
            dma((7,)),
            dma((2,)),
            dma((8,)),
            dma((8,)),
            dma((20,)),
            dma((20,)),
            dma((3,)),
            dma((3,)),
            dma((4,)),
            dma((4,)),
            pltpu.SemaphoreType.REGULAR,
        ],
        compiler_params=pltpu.CompilerParams(
            collective_id=0, has_side_effects=True, vmem_limit_bytes=56 * 2**20
        ),
        cost_estimate=pl.CostEstimate(
            flops=100_000_000, bytes_accessed=7_000_000, transcendentals=40_000
        ),
    )(
        fold(populations),
        fold(kinds),
        fold(temperature),
        lines,
        wanted[0].T,
        places,
        hits,
        beam[0],
    )
    return unfold(lattice), unfold(heated)


def solution(mesh):
    placed = (
        P(None, "gz", "gy"),
        P("gz", "gy"),
        P("gz", "gy"),
        P(("gz", "gy"), None),
        P(("gz", "gy"), None, None),
        P(("gz", "gy"), None),
        P(("gz", "gy"), None),
        P(("gz", "gy"), None, None),
    )
    return jax.shard_map(
        per_device,
        mesh=mesh,
        in_specs=placed,
        out_specs=(P(None, "gz", "gy"), P("gz", "gy")),
        check_vma=False,
    )
```

profile of v0, /device:TPU:0, one launch (start us, length us, event | category | flops | bytes accessed | tf_op | source)
XLA Modules:
  0.0 61.3 jit_solution(17339275477723088513)
XLA Ops:
  0.6 56.4 %shard_map.95 = (f32[19,288,128]{2,1,0:T(8,128)}, f32[288,128]{1,0:T(8,128)}) custom-call(f32[19,288,128]{2,1,0:T(8,128)} %bitcast.29, s32[288,128]{1,0:T(8,128)} %bitcast.31, f32[288,128]{1,0:T(8,128)} %bitcast.32, s32[1,64]{1,0:T(1,128)} %line_hbm.1, s32[4,128]{1,0:T(4,128)} %bitcast.35, s32[1,512]{1,0:T(1,128)} %place_hbm.1, s32[1,64]{1,0:T(1,128)} %hits_hbm.1, ...), custom_call_target="tpu_custom_call" | custom-call | flops 100000000 | bytes 7000000 | tf_op jit(solution)/shard_map/pallas_call | solution.py:595
  57.0 0.0 copy-start
  57.0 3.6 %copy.17 = f32[19,4,9216]{2,1,0:T(4,128)} copy(f32[19,4,9216]{2,1,0:T(4,128)} %bitcast.30) | data formatting | bytes 5603328
  60.6 0.0 copy-done
  60.6 0.7 %copy.18 = f32[4,9216]{1,0:T(4,128)} copy(f32[4,9216]{1,0:T(4,128)S(1)} %bitcast.33) | data formatting | bytes 294912
Async XLA Ops:
  57.0 3.6 %copy-start = (f32[288,128]{1,0:T(8,128)S(1)}, f32[288,128]{1,0:T(8,128)}, u32[]{:S(2)}) copy-start(f32[288,128]{1,0:T(8,128)} %get-tuple-element.5) | copy-start | bytes 442372
where the time goes:
time: 62.3 us; the launch traced here: 61.3 us
  Pallas kernels  56.4 us (91%)
  local copies, waits for them, and re-layouts  4.24 us (7%)
  between operations  0.65 us (1%)
    pallas_call x1, Pallas kernels, per_device(): pl.pallas_call(kernel, out_shape=(jax.ShapeDtypeStruct((19, CELL_ROWS, 12...  56.4 us
    unnamed x4, local copies, waits for them, and re-layouts  4.24 us

commit v1 on v0

--- a/solution.py
+++ b/solution.py
@@ -166,16 +166,28 @@
     return both[:, :128] + both[:, 128:]
 
 
-def edge_tile(j):
-    late = lax.div(j, 18)
-    k = j - 18
-    z = (1 - late) * (lax.div(j, 9) * 3) + late * (1 + lax.div(k, 2))
-    rb = (1 - late) * lax.rem(j, 9) + late * (lax.rem(k, 2) * 8)
-    return z, rb
-
-
 def inner_tile(j):
     return 1 + lax.div(j, 7), 1 + lax.rem(j, 7)
+
+
+def side_tile(j):
+    return 1 + lax.div(j, 2), lax.rem(j, 2) * 8
+
+
+def face_tile(third):
+    return lambda j: (lax.div(j, 3) * 3, third * 3 + lax.rem(j, 3))
+
+
+def any_tile(j):
+    return lax.div(j, 9), lax.rem(j, 9)
+
+
+def over(tile, count, body, unroll=None):
+    def step(j, carry):
+        body(*tile(j))
+        return carry
+
+    lax.fori_loop(0, count, step, 0, unroll=unroll or count)
 
 
 def kernel(
@@ -187,9 +199,10 @@
     place_hbm,
     hits_hbm,
     beam_hbm,
-    out_hbm,
-    temp_out_hbm,
     field,
+    thermal,
+    cells,
+    inputs,
     kind,
     temp,
     line,
@@ -202,7 +215,6 @@
     post2,
     mask,
     vel,
-    cells,
     ask_send,
     ask_recv,
     row_send,
@@ -215,11 +227,8 @@
     back_hot,
     ray_rows,
     live,
-    thermal,
-    temp_out,
     load_sem,
     small_sem,
-    out_sem,
     gas_s,
     gas_r,
     halo_s,
@@ -268,9 +277,7 @@
 
     def part(rb):
         rows = pl.ds(rb * 32, 32)
-        return pltpu.make_async_copy(
-            pop_hbm.at[:, rows], field.at[:, rows], load_sem.at[rb]
-        )
+        return pltpu.make_async_copy(pop_hbm.at[:, rows], inputs.at[:, rows], load_sem.at[rb])
 
     def start_part(rb, carry):
         part(rb).start()
@@ -279,22 +286,11 @@
     lax.fori_loop(0, 9, start_part, 0)
     small[0].wait()
 
-    def first(rb, carry):
-        part(rb).wait()
-        for z in range(DEPTH):
-            rows = pl.ds(rb * 32 + z, 8, stride=DEPTH)
-            gas = kind[rows, :] == 0
-            gas_pad[z + 1, pl.ds(rb * 8 + PAD, 8), :] = gas.astype(jnp.int32)
-            kept, velocity = collide([field[q, rows, :] for q in range(19)], gas)
-            for q in range(19):
-                post1[SLOT[q], z + 1, pl.ds(rb * 8 + PAD, 8), :] = kept[q]
-            for i in range(4):
-                vel[i, z, pl.ds(rb * 8, 8), :] = velocity[i]
-        return carry
-
-    lax.fori_loop(0, 9, first, 0)
-
-    pl.semaphore_wait(barrier, N_GZ - 1 + N_GY - 1 + 4)
+    def flags(z, rb):
+        gas = kind[pl.ds(rb * 32 + z, 8, stride=DEPTH), :] == 0
+        gas_pad[z + 1, pl.ds(rb * 8 + PAD, 8), :] = gas.astype(jnp.int32)
+
+    over(any_tile, 36, flags, 12)
 
     low_src, low_dst = slice(PAD, PAD + 2), slice(PAD + ROWS, PAD + ROWS + 2)
     high_src, high_dst = slice(PAD + ROWS - 2, PAD + ROWS), slice(PAD - 2, PAD)
@@ -313,21 +309,29 @@
         copy.start()
         return copy
 
-    def halo(ref, first_sem):
-        moves = (
-            ((slice(0, 5), 4, body), (slice(0, 5), 0, body), (up, gy)),
-            ((slice(5, 10), 1, body), (slice(5, 10), 5, body), (down, gy)),
-            ((slice(4, 6), planes, high_src), (slice(4, 6), planes, high_dst), (gz, north)),
-            ((slice(16, 19), planes, high_src), (slice(16, 19), planes, high_dst), (gz, north)),
-            ((slice(9, 13), planes, low_src), (slice(9, 13), planes, low_dst), (gz, south)),
-            ((slice(0, 1), planes, low_src), (slice(0, 1), planes, low_dst), (gz, south)),
-            ((4, 4, high_src), (4, 0, high_dst), (up, north)),
-            ((9, 1, low_src), (9, 5, low_dst), (down, south)),
-            ((5, 1, high_src), (5, 5, high_dst), (down, north)),
-            ((0, 4, low_src), (0, 0, low_dst), (up, south)),
+    def face_moves(third):
+        rows = slice(PAD + 24 * third, PAD + 24 * third + 24)
+        return (
+            ((slice(0, 5), 4, rows), (slice(0, 5), 0, rows), (up, gy)),
+            ((slice(5, 10), 1, rows), (slice(5, 10), 5, rows), (down, gy)),
         )
+
+    side_moves = (
+        ((slice(4, 6), planes, high_src), (slice(4, 6), planes, high_dst), (gz, north)),
+        ((slice(16, 19), planes, high_src), (slice(16, 19), planes, high_dst), (gz, north)),
+        ((slice(9, 13), planes, low_src), (slice(9, 13), planes, low_dst), (gz, south)),
+        ((slice(0, 1), planes, low_src), (slice(0, 1), planes, low_dst), (gz, south)),
+    )
+    corner_moves = (
+        ((4, 4, high_src), (4, 0, high_dst), (up, north)),
+        ((9, 1, low_src), (9, 5, low_dst), (down, south)),
+        ((5, 1, high_src), (5, 5, high_dst), (down, north)),
+        ((0, 4, low_src), (0, 0, low_dst), (up, south)),
+    )
+
+    def send_all(ref, moves, s, r, first_sem):
         return [
-            send(ref, src, dst, halo_s.at[first_sem + i], halo_r.at[first_sem + i], peer)
+            send(ref, src, dst, s.at[first_sem + i], r.at[first_sem + i], peer)
             for i, (src, dst, peer) in enumerate(moves)
         ]
 
@@ -341,11 +345,29 @@
         ((1, high_src), (5, high_dst), (down, north)),
         ((1, low_src), (5, low_dst), (down, south)),
     )
-    gas_copies = [
-        send(gas_pad, src, dst, gas_s.at[i], gas_r.at[i], peer)
-        for i, (src, dst, peer) in enumerate(gas_moves)
-    ]
-    copies1 = halo(post1, 0)
+
+    def first(z, rb):
+        rows = pl.ds(rb * 32 + z, 8, stride=DEPTH)
+        kept, velocity = collide([inputs[q, rows, :] for q in range(19)], kind[rows, :] == 0)
+        for q in range(19):
+            post1[SLOT[q], z + 1, pl.ds(rb * 8 + PAD, 8), :] = kept[q]
+        for i in range(4):
+            vel[i, z, pl.ds(rb * 8, 8), :] = velocity[i]
+
+    faces1, gas_copies = [], []
+    for third in range(3):
+        for rb in range(3 * third, 3 * third + 3):
+            part(rb).wait()
+        over(lambda j: (lax.div(j, 3), 3 * third + lax.rem(j, 3)), 12, first)
+        if third == 0:
+            pl.semaphore_wait(barrier, N_GZ - 1 + N_GY - 1 + 4)
+        faces1 += send_all(post1, face_moves(third), halo_s, halo_r, 2 * third)
+        if third == 0:
+            gas_copies += send_all(gas_pad, gas_moves[:2], gas_s, gas_r, 0)
+        if third == 1:
+            gas_copies += send_all(gas_pad, gas_moves[2:], gas_s, gas_r, 2)
+    sides1 = send_all(post1, side_moves, halo_s, halo_r, 6)
+    corners1 = send_all(post1, corner_moves, halo_s, halo_r, 10)
 
     for i in range(1, N_GY):
         pl.semaphore_signal(row_sem, 1, device_id=(gz, lax.rem(gy + i, N_GY)), device_id_type=MESH)
@@ -364,8 +386,15 @@
     pl.semaphore_wait(row_sem, N_GY - 1)
 
     def peer_of(i):
-        p = lax.rem(me + i, DEVICES)
-        return p, (lax.div(p, N_GY), lax.rem(p, N_GY))
+        def onward(own, k):
+            return lax.rem(own + 10 - lax.div(k * (k + 1), 2), 4)
+
+        x = onward(lax.div(gz, 8), lax.div(i, 32))
+        y = onward(lax.rem(lax.div(gz, 2), 4), lax.rem(lax.div(i, 8), 4))
+        z = onward(gy, lax.rem(lax.div(i, 2), 4))
+        core = lax.rem(gz + 1 + lax.rem(i, 2), 2)
+        column = (x * 4 + y) * 2 + core
+        return column * N_GY + z, (column, z)
 
     def ask(i, carry):
         p, peer = peer_of(i)
@@ -379,13 +408,9 @@
         ).start()
         return carry
 
-    lax.fori_loop(1, DEVICES, ask, 0)
-
-    for copy in gas_copies:
-        copy.wait()
-
-    def masks(j, carry):
-        z, rb = lax.div(j, 9), lax.rem(j, 9)
+    lax.fori_loop(0, DEVICES - 1, ask, 0)
+
+    def masks(z, rb):
         place_x = lax.rem(
             (rb * 8 + tile_iota(0)) * 128 + tile_iota(1), jnp.full((8, 128), ACROSS, jnp.int32)
         )
@@ -398,28 +423,33 @@
             bits = bits | (jnp.maximum(source, own) << q)
         bits = bits | (left.astype(jnp.int32) << LEFT_BIT) | (right.astype(jnp.int32) << RIGHT_BIT)
         mask[z, pl.ds(rb * 8, 8), :] = bits
-        return carry
-
-    lax.fori_loop(0, 36, masks, 0)
-
-    def second(tile):
-        def step(j, carry):
-            z, rb = tile(j)
-            new, gas = passed(post1, mask, vel, z, rb)
-            kept, velocity = collide(new, gas)
-            for q in range(19):
-                post2[SLOT[q], z + 1, pl.ds(rb * 8 + PAD, 8), :] = kept[q]
-            for i in range(4):
-                vel[i, z, pl.ds(rb * 8, 8), :] = velocity[i]
-            return carry
-
-        return step
-
-    lax.fori_loop(0, 14, second(inner_tile), 0)
-    for copy in copies1:
+
+    def second(z, rb):
+        new, gas = passed(post1, mask, vel, z, rb)
+        kept, velocity = collide(new, gas)
+        for q in range(19):
+            post2[SLOT[q], z + 1, pl.ds(rb * 8 + PAD, 8), :] = kept[q]
+        for i in range(4):
+            vel[i, z, pl.ds(rb * 8, 8), :] = velocity[i]
+
+    over(inner_tile, 14, masks, 7)
+    over(inner_tile, 14, second, 7)
+    for copy in gas_copies:
         copy.wait()
-    lax.fori_loop(0, 22, second(edge_tile), 0)
-    copies2 = halo(post2, 10)
+    over(side_tile, 4, masks)
+    for third in range(3):
+        over(face_tile(third), 6, masks)
+    for copy in sides1:
+        copy.wait()
+    over(side_tile, 4, second)
+    for copy in faces1 + corners1:
+        copy.wait()
+    faces2 = []
+    for third in range(3):
+        over(face_tile(third), 6, second)
+        faces2 += send_all(post2, face_moves(third), halo_s, halo_r, 14 + 2 * third)
+    corners2 = send_all(post2, corner_moves, halo_s, halo_r, 24)
+    sides2 = send_all(post2, side_moves, halo_s, halo_r, 20)
 
     big0, big1 = tile_iota(0, (SLOTS, SLOTS)), tile_iota(1, (SLOTS, SLOTS))
     diagonal = big0 == big1
@@ -458,33 +488,30 @@
     )
     cells[CELL_ROWS:, :] = jnp.zeros((384 - CELL_ROWS, 128), jnp.float32)
 
-    def third(tile):
-        def step(j, carry):
-            z, rb = tile(j)
-            new, gas = passed(post2, mask, vel, z, rb)
-            rows = pl.ds(rb * 32 + z, 8, stride=DEPTH)
-            for q in range(19):
-                field[q, rows, :] = new[q]
-            density, ux, uy, uz = moments(new)
-            for i, v in enumerate((ux, uy, uz)):
-                vel[i, z, pl.ds(rb * 8, 8), :] = v
-            cosine = 0.2 + 0.7 / (1.0 + jnp.exp(-8.0 * (density - 1.0)))
-            index = 1.0 + temp[rows, :]
-            upper = (index - cosine) * (index - cosine) + 1.0
-            lower = (index + cosine) * (index + cosine) + 1.0
-            cells[pl.ds(pl.multiple_of(z * ROWS + rb * 8, 8), 8), :] = jnp.where(
-                gas, 1.0, upper / lower
-            )
-            return carry
-
-        return step
-
-    lax.fori_loop(0, 14, third(inner_tile), 0)
-    for copy in copies2:
+    def last(z, rb):
+        new, gas = passed(post2, mask, vel, z, rb)
+        rows = pl.ds(rb * 32 + z, 8, stride=DEPTH)
+        for q in range(19):
+            field[q, rows, :] = new[q]
+        density, ux, uy, uz = moments(new)
+        for i, v in enumerate((ux, uy, uz)):
+            vel[i, z, pl.ds(rb * 8, 8), :] = v
+        cosine = 0.2 + 0.7 / (1.0 + jnp.exp(-8.0 * (density - 1.0)))
+        index = 1.0 + temp[rows, :]
+        upper = (index - cosine) * (index - cosine) + 1.0
+        lower = (index + cosine) * (index + cosine) + 1.0
+        cells[pl.ds(pl.multiple_of(z * ROWS + rb * 8, 8), 8), :] = jnp.where(
+            gas, 1.0, upper / lower
+        )
+
+    over(inner_tile, 14, last, 7)
+    for copy in sides2:
         copy.wait()
-    lax.fori_loop(0, 22, third(edge_tile), 0)
-    lattice_copy = pltpu.make_async_copy(field, out_hbm, out_sem.at[0])
-    lattice_copy.start()
+    over(side_tile, 4, last)
+    for copy in faces2 + corners2:
+        copy.wait()
+    for third in range(3):
+        over(face_tile(third), 6, last)
 
     def to_all(src, dst, n):
         dst[:, pl.ds(me, 1), :] = src[:, pl.ds(me, 1), :]
@@ -501,7 +528,7 @@
             ).start()
             return carry
 
-        lax.fori_loop(1, DEVICES, one, 0)
+        lax.fori_loop(0, DEVICES - 1, one, 0)
         pltpu.make_async_copy(
             src.at[:, pl.ds(0, DEVICES - 1)], dst.at[:, pl.ds(0, DEVICES - 1)], all_r.at[n]
         ).wait()
@@ -522,37 +549,45 @@
 
     cells[pl.ds(0, CELL_ROWS), :] = pick(back_hot[...], heat_recv[...].reshape(SLOTS, 128))
 
-    def sources(j, carry):
-        z, rb = lax.div(j, 9), lax.rem(j, 9)
-        deposit = cells[pl.ds(pl.multiple_of(z * ROWS + rb * 8, 8), 8), :]
-        source = temp[pl.ds(rb * 32 + z, 8, stride=DEPTH), :] + deposit
+    def sources(z, rb):
+        at = pl.ds(pl.multiple_of(z * ROWS + rb * 8, 8), 8)
+        source = temp[pl.ds(rb * 32 + z, 8, stride=DEPTH), :] + cells[at, :]
         eighth = 0.125 * source
         for i in range(3):
             moved = eighth * (4.0 * vel[i, z, pl.ds(rb * 8, 8), :])
             thermal[2 * i, z + 1, pl.ds(rb * 8 + PAD, 8), :] = eighth + moved
             thermal[2 * i + 1, z + 1, pl.ds(rb * 8 + PAD, 8), :] = eighth - moved
-        cells[pl.ds(pl.multiple_of(z * ROWS + rb * 8, 8), 8), :] = 0.25 * source
-        return carry
-
-    lax.fori_loop(0, 36, sources, 0)
+        cells[at, :] = 0.25 * source
+
+    over(any_tile, 36, sources, 12)
     th_moves = (
         ((4, 4, body), (4, 0, body), (up, gy)),
         ((5, 1, body), (5, 5, body), (down, gy)),
         ((2, planes, high_src), (2, planes, high_dst), (gz, north)),
         ((3, planes, low_src), (3, planes, low_dst), (gz, south)),
     )
-    th_copies = [
-        send(thermal, src, dst, th_s.at[i], th_r.at[i], peer)
-        for i, (src, dst, peer) in enumerate(th_moves)
-    ]
-    for copy in th_copies:
+    for copy in send_all(thermal, th_moves, th_s, th_r, 0):
         copy.wait()
-
-    def gather(j, carry):
-        z, rb = lax.div(j, 9), lax.rem(j, 9)
-        bits = mask[z, pl.ds(rb * 8, 8), :]
-        left = (bits & (1 << LEFT_BIT)) != 0
-        right = (bits & (1 << RIGHT_BIT)) != 0
+    pltpu.make_async_copy(
+        ask_send.at[pl.ds(0, DEVICES - 1)], ask_recv.at[pl.ds(0, DEVICES - 1)], all_s.at[0]
+    ).wait()
+    for n, ref in ((1, row_send), (2, heat_send)):
+        done = ref.at[:, pl.ds(0, DEVICES - 1)]
+        pltpu.make_async_copy(done, done, all_s.at[n]).wait()
+
+
+def finish(field, thermal, cells, out_hbm, temp_out_hbm, temp_out, out_sem, temp_sem):
+    copies = []
+    for i, (lo, hi) in enumerate(((0, 5), (5, 10), (10, 15), (15, 19))):
+        copy = pltpu.make_async_copy(field.at[lo:hi], out_hbm.at[lo:hi], out_sem.at[i])
+        copy.start()
+        copies.append(copy)
+
+    def gather(z, rb):
+        place_x = lax.rem(
+            (rb * 8 + tile_iota(0)) * 128 + tile_iota(1), jnp.full((8, 128), ACROSS, jnp.int32)
+        )
+        left, right = place_x == 0, place_x == ACROSS - 1
         total = cells[pl.ds(pl.multiple_of(z * ROWS + rb * 8, 8), 8), :]
         for i in range(6):
             step_x, step_y, step_z = DIRS[i + 1]
@@ -560,19 +595,13 @@
                 window(thermal, (i,), z + 1 - step_z, rb), step_x, step_y, left, right
             )
         temp_out[pl.ds(rb * 32 + z, 8, stride=DEPTH), :] = total
-        return carry
-
-    lax.fori_loop(0, 36, gather, 0)
-    last = pltpu.make_async_copy(temp_out, temp_out_hbm, out_sem.at[1])
-    last.start()
-    last.wait()
-    lattice_copy.wait()
-    pltpu.make_async_copy(
-        ask_send.at[pl.ds(0, DEVICES - 1)], ask_recv.at[pl.ds(0, DEVICES - 1)], all_s.at[0]
-    ).wait()
-    for n, ref in ((1, row_send), (2, heat_send)):
-        done = ref.at[:, pl.ds(0, DEVICES - 1)]
-        pltpu.make_async_copy(done, done, all_s.at[n]).wait()
+
+    over(lambda j: (lax.rem(j, 4), lax.div(j, 4)), 36, gather, 12)
+    copy = pltpu.make_async_copy(temp_out, temp_out_hbm, temp_sem)
+    copy.start()
+    copy.wait()
+    for copy in copies:
+        copy.wait()
 
 
 def fold(x):
@@ -592,14 +621,27 @@
 def per_device(populations, kinds, temperature, lines, wanted, places, hits, beam):
     f32, i32, bf16 = jnp.float32, jnp.int32, jnp.bfloat16
     dma = pltpu.SemaphoreType.DMA
-    lattice, heated = pl.pallas_call(
+    vmem = pl.BlockSpec(memory_space=pltpu.VMEM)
+    whole = pl.BlockSpec(memory_space=pl.ANY)
+    operands = (
+        fold(populations),
+        fold(kinds),
+        fold(temperature),
+        lines,
+        wanted[0].T,
+        places,
+        hits,
+        beam[0],
+    )
+    field, thermal, cells = pl.pallas_call(
         kernel,
         out_shape=(
-            jax.ShapeDtypeStruct((19, CELL_ROWS, 128), f32),
-            jax.ShapeDtypeStruct((CELL_ROWS, 128), f32),
+            pltpu.VMEM((19, CELL_ROWS, 128), f32),
+            pltpu.VMEM((6, DEPTH + 2, PLANE, 128), f32),
+            pltpu.VMEM((384, 128), f32),
         ),
-        in_specs=[pl.BlockSpec(memory_space=pl.ANY)] * 8,
-        out_specs=[pl.BlockSpec(memory_space=pl.ANY)] * 2,
+        in_specs=[whole] * 8,
+        out_specs=[vmem] * 3,
         scratch_shapes=[
             pltpu.VMEM((19, CELL_ROWS, 128), f32),
             pltpu.VMEM((CELL_ROWS, 128), i32),
@@ -614,7 +656,6 @@
             pltpu.VMEM((19, DEPTH + 2, PLANE, 128), f32),
             pltpu.VMEM((DEPTH, ROWS, 128), i32),
             pltpu.VMEM((4, DEPTH, ROWS, 128), f32),
-            pltpu.VMEM((384, 128), f32),
             pltpu.VMEM((DEVICES, 128), f32),
             pltpu.VMEM((DEVICES, 128), f32),
             pltpu.VMEM((CAP, DEVICES, 128), f32),
@@ -627,15 +668,12 @@
             pltpu.VMEM((CELL_ROWS, SLOTS), bf16),
             pltpu.VMEM((SLOTS, 128), f32),
             pltpu.VMEM((RAYS, 128), f32),
-            pltpu.VMEM((6, DEPTH + 2, PLANE, 128), f32),
-            pltpu.VMEM((CELL_ROWS, 128), f32),
             dma((9,)),
             dma((7,)),
-            dma((2,)),
             dma((8,)),
             dma((8,)),
-            dma((20,)),
-            dma((20,)),
+            dma((28,)),
+            dma((28,)),
             dma((3,)),
             dma((3,)),
             dma((4,)),
@@ -643,21 +681,26 @@
             pltpu.SemaphoreType.REGULAR,
         ],
         compiler_params=pltpu.CompilerParams(
-            collective_id=0, has_side_effects=True, vmem_limit_bytes=56 * 2**20
+            collective_id=0, has_side_effects=True, vmem_limit_bytes=40 * 2**20
         ),
         cost_estimate=pl.CostEstimate(
             flops=100_000_000, bytes_accessed=7_000_000, transcendentals=40_000
         ),
-    )(
-        fold(populations),
-        fold(kinds),
-        fold(temperature),
-        lines,
-        wanted[0].T,
-        places,
-        hits,
-        beam[0],
-    )
+    )(*[pltpu.with_memory_space_constraint(x, pltpu.HBM) for x in operands])
+    lattice, heated = pl.pallas_call(
+        finish,
+        out_shape=(
+            jax.ShapeDtypeStruct((19, CELL_ROWS, 128), f32),
+            jax.ShapeDtypeStruct((CELL_ROWS, 128), f32),
+        ),
+        in_specs=[vmem] * 3,
+        out_specs=[whole] * 2,
+        scratch_shapes=[pltpu.VMEM((CELL_ROWS, 128), f32), dma((4,)), dma],
+        compiler_params=pltpu.CompilerParams(vmem_limit_bytes=40 * 2**20),
+        cost_estimate=pl.CostEstimate(
+            flops=1_000_000, bytes_accessed=7_000_000, transcendentals=0
+        ),
+    )(*[pltpu.with_memory_space_constraint(x, pltpu.VMEM) for x in (field, thermal, cells)])
     return unfold(lattice), unfold(heated)
 
 

time: 62.3 us -> 50.7 us (0.81); the launches traced: 61.3 us -> 50.6 us
  Pallas kernels: 56.4 us -> 49.9 us
  local copies, waits for them, and re-layouts: 4.24 us -> 0 us
    pallas_call x1 -> x2, Pallas kernels: 56.4 us -> 49.9 us  [the longest x1 48.3 us: per_device(): pl.pallas_call(kernel, out_shape=(pltpu.VMEM((19, CELL_ROWS, 128), f32),...]
    unnamed x4 -> x0, local copies, waits for them, and re-layouts: 4.24 us -> none
where the time goes in v1:
time: 50.7 us; the launch traced here: 50.6 us
  Pallas kernels  49.9 us (98%)
  between operations  0.64 us (1%)
    pallas_call x1, Pallas kernels, per_device(): pl.pallas_call(kernel, out_shape=(pltpu.VMEM((19, CELL_ROWS, 128), f32),...  48.3 us
    pallas_call x1, Pallas kernels, per_device(): pl.pallas_call(finish, out_shape=(jax.ShapeDtypeStruct((19, CELL_ROWS, 12...  1.64 us

profile of v1, /device:TPU:0, one launch (start us, length us, event | category | flops | bytes accessed | tf_op | source)
XLA Modules:
  0.0 50.6 jit_solution(13394347290065616361)
XLA Ops:
  0.6 48.3 %shard_map.95 = (f32[19,288,128]{2,1,0:T(8,128)S(1)}, f32[6,6,88,128]{3,2,1,0:T(8,128)S(1)}, f32[384,128]{1,0:T(8,128)S(1)}) custom-call(f32[19,288,128]{2,1,0:T(8,128)} %bitcast.29, s32[288,128]{1,0:T(8,128)} %bitcast.30, f32[288,128]{1,0:T(8,128)} %bitcast.31, s32[1,64]{1,0:T(1,128)} %line_hbm.1, s32[4,128]{1,0:T(4,128)} %bitcast.33, s32[1,512]{1,0:T(1,128)} %place_hbm.1, ...), custom_call_target="tpu_custom_call" | custom-call | flops 100000000 | bytes 7000000 | tf_op jit(solution)/shard_map/pallas_call | solution.py:636
  48.9 1.6 %shard_map.96 = (f32[19,288,128]{2,1,0:T(8,128)}, f32[288,128]{1,0:T(8,128)}) custom-call(f32[19,288,128]{2,1,0:T(8,128)S(1)} %get-tuple-element.7.field, f32[6,6,88,128]{3,2,1,0:T(8,128)S(1)} %get-tuple-element.8.thermal, f32[384,128]{1,0:T(8,128)S(1)} %get-tuple-element.9.cells), custom_call_target="tpu_custom_call" | custom-call | flops 1000000 | bytes 7000000 | tf_op jit(solution)/shard_map/pallas_call | solution.py:690

commit v2 on v1

--- a/solution.py
+++ b/solution.py
@@ -216,6 +216,7 @@
     mask,
     vel,
     ask_send,
+    ask_mid,
     ask_recv,
     row_send,
     row_recv,
@@ -237,32 +238,28 @@
     all_r,
     th_s,
     th_r,
-    row_sem,
 ):
     gz = lax.axis_index("gz")
     gy = lax.axis_index("gy")
-    me = gz * N_GY + gy
     up, down = lax.rem(gz + 1, N_GZ), lax.rem(gz + N_GZ - 1, N_GZ)
     north, south = lax.rem(gy + 1, N_GY), lax.rem(gy + N_GY - 1, N_GY)
 
-    barrier = pltpu.get_barrier_semaphore()
-
-    def greet(i, carry):
-        pl.semaphore_signal(
-            barrier, 1, device_id=(lax.rem(gz + i, N_GZ), gy), device_id_type=MESH
-        )
+    kind_copy = pltpu.make_async_copy(kind_hbm, kind, small_sem.at[6])
+    kind_copy.start()
+
+    def part(rb):
+        rows = pl.ds(rb * 32, 32)
+        return pltpu.make_async_copy(pop_hbm.at[:, rows], inputs.at[:, rows], load_sem.at[rb])
+
+    def start_part(rb, carry):
+        part(rb).start()
         return carry
 
-    lax.fori_loop(1, N_GZ, greet, 0)
-    for i in range(1, N_GY):
-        pl.semaphore_signal(barrier, 1, device_id=(gz, lax.rem(gy + i, N_GY)), device_id_type=MESH)
-    for peer in ((up, north), (up, south), (down, north), (down, south)):
-        pl.semaphore_signal(barrier, 1, device_id=peer, device_id_type=MESH)
+    lax.fori_loop(0, 9, start_part, 0, unroll=9)
 
     small = []
     for i, (src, dst) in enumerate(
         (
-            (kind_hbm, kind),
             (want_hbm, want),
             (line_hbm, line),
             (place_hbm, place),
@@ -275,16 +272,21 @@
         copy.start()
         small.append(copy)
 
-    def part(rb):
-        rows = pl.ds(rb * 32, 32)
-        return pltpu.make_async_copy(pop_hbm.at[:, rows], inputs.at[:, rows], load_sem.at[rb])
-
-    def start_part(rb, carry):
-        part(rb).start()
+    barrier = pltpu.get_barrier_semaphore()
+
+    def greet(i, carry):
+        pl.semaphore_signal(
+            barrier, 1, device_id=(lax.rem(gz + i, N_GZ), gy), device_id_type=MESH
+        )
         return carry
 
-    lax.fori_loop(0, 9, start_part, 0)
-    small[0].wait()
+    lax.fori_loop(1, N_GZ, greet, 0, unroll=N_GZ - 1)
+    for i in range(1, N_GY):
+        pl.semaphore_signal(barrier, 1, device_id=(gz, lax.rem(gy + i, N_GY)), device_id_type=MESH)
+    for peer in ((up, north), (up, south), (down, north), (down, south)):
+        pl.semaphore_signal(barrier, 1, device_id=peer, device_id_type=MESH)
+
+    kind_copy.wait()
 
     def flags(z, rb):
         gas = kind[pl.ds(rb * 32 + z, 8, stride=DEPTH), :] == 0
@@ -369,46 +371,47 @@
     sides1 = send_all(post1, side_moves, halo_s, halo_r, 6)
     corners1 = send_all(post1, corner_moves, halo_s, halo_r, 10)
 
-    for i in range(1, N_GY):
-        pl.semaphore_signal(row_sem, 1, device_id=(gz, lax.rem(gy + i, N_GY)), device_id_type=MESH)
-
-    for copy in small[1:]:
+    for copy in small:
         copy.wait()
-    eye = tile_iota(0, (DEVICES, DEVICES)) == tile_iota(1, (DEVICES, DEVICES))
-    lanes = tile_iota(1, (DEVICES, DEVICES))
+    row, lane = tile_iota(0, (DEVICES, DEVICES)), tile_iota(1, (DEVICES, DEVICES))
+    holder = lane == (row & (N_GZ - 1)) * N_GY + (row >> 5)
     rows_of = jnp.zeros((DEVICES, DEVICES), jnp.float32)
     for s in range(CAP):
         asked = want[s : s + 1, :].astype(jnp.float32)
-        column = jnp.sum(jnp.where(eye, asked, 0.0), axis=1, keepdims=True)
-        rows_of = jnp.where(lanes == s, column, rows_of)
-    ask_send[...] = rows_of
-    ask_recv[pl.ds(me, 1), :] = ask_send[pl.ds(me, 1), :]
-    pl.semaphore_wait(row_sem, N_GY - 1)
-
-    def peer_of(i):
-        def onward(own, k):
-            return lax.rem(own + 10 - lax.div(k * (k + 1), 2), 4)
-
-        x = onward(lax.div(gz, 8), lax.div(i, 32))
-        y = onward(lax.rem(lax.div(gz, 2), 4), lax.rem(lax.div(i, 8), 4))
-        z = onward(gy, lax.rem(lax.div(i, 2), 4))
-        core = lax.rem(gz + 1 + lax.rem(i, 2), 2)
-        column = (x * 4 + y) * 2 + core
-        return column * N_GY + z, (column, z)
-
-    def ask(i, carry):
-        p, peer = peer_of(i)
+        column = jnp.sum(jnp.where(holder, asked, 0.0), axis=1, keepdims=True)
+        rows_of = jnp.where(lane == s, column, rows_of)
+    ask_send[...] = rows_of.reshape(N_GY, N_GZ, DEVICES)
+    ask_mid[gy] = ask_send[gy]
+    for i in range(1, N_GY):
+        peer = lax.rem(gy + i, N_GY)
         pltpu.make_async_remote_copy(
-            src_ref=ask_send.at[pl.ds(p, 1)],
-            dst_ref=ask_recv.at[pl.ds(me, 1)],
+            src_ref=ask_send.at[peer],
+            dst_ref=ask_mid.at[gy],
             send_sem=all_s.at[0],
             recv_sem=all_r.at[0],
-            device_id=peer,
+            device_id=(gz, peer),
             device_id_type=MESH,
         ).start()
-        return carry
-
-    lax.fori_loop(0, DEVICES - 1, ask, 0)
+
+    def ask_columns():
+        pltpu.make_async_copy(
+            ask_send.at[: N_GY - 1], ask_mid.at[: N_GY - 1], all_r.at[0]
+        ).wait()
+        ask_recv[:, pl.ds(gz, 1), :] = ask_mid[:, pl.ds(gz, 1), :]
+
+        def ask(i, carry):
+            peer = lax.rem(gz + i, N_GZ)
+            pltpu.make_async_remote_copy(
+                src_ref=ask_mid.at[:, pl.ds(peer, 1)],
+                dst_ref=ask_recv.at[:, pl.ds(gz, 1)],
+                send_sem=all_s.at[3],
+                recv_sem=all_r.at[3],
+                device_id=(peer, gy),
+                device_id_type=MESH,
+            ).start()
+            return carry
+
+        lax.fori_loop(1, N_GZ, ask, 0, unroll=N_GZ - 1)
 
     def masks(z, rb):
         place_x = lax.rem(
@@ -434,6 +437,7 @@
 
     over(inner_tile, 14, masks, 7)
     over(inner_tile, 14, second, 7)
+    ask_columns()
     for copy in gas_copies:
         copy.wait()
     over(side_tile, 4, masks)
@@ -454,7 +458,7 @@
     big0, big1 = tile_iota(0, (SLOTS, SLOTS)), tile_iota(1, (SLOTS, SLOTS))
     diagonal = big0 == big1
     spot = place[...]
-    spot = (spot & 3) * DEVICES + (spot >> 2)
+    spot = (spot & 3) * DEVICES + ((spot >> 2) & 3) * N_GZ + (spot >> 4)
     slot_hot[...] = (big0 == spot).astype(jnp.float32).astype(jnp.bfloat16)
     spot_col = jnp.sum(
         jnp.where(diagonal, spot.astype(jnp.float32), 0.0), axis=1, keepdims=True
@@ -465,14 +469,14 @@
         jnp.sum(jnp.where(eye_rays, hits[...].astype(jnp.float32), 0.0), axis=1, keepdims=True),
         (RAYS, 128),
     )
-    pltpu.make_async_copy(
-        ask_send.at[pl.ds(0, DEVICES - 1)], ask_recv.at[pl.ds(0, DEVICES - 1)], all_r.at[0]
-    ).wait()
+    others = ask_recv.at[:, : N_GZ - 1]
+    pltpu.make_async_copy(others, others, all_r.at[3]).wait()
+    asked_rows = ask_recv[...].reshape(DEVICES, DEVICES)
     block = tile_iota(1, (DEVICES, NB_DEV)).astype(jnp.float32)
     lines = line[...].astype(jnp.float32)
     wanted_row = []
     for s in range(CAP):
-        chosen = ask_recv[:, s : s + 1] == block
+        chosen = asked_rows[:, s : s + 1] == block
         wanted_row.append(jnp.sum(jnp.where(chosen, lines, 0.0), axis=1, keepdims=True))
     row_col = jnp.concatenate(wanted_row, axis=0)
     cell_hot[...] = (
@@ -513,22 +517,42 @@
     for third in range(3):
         over(face_tile(third), 6, last)
 
+    place_x, place_y = lax.div(gz, 8), lax.rem(lax.div(gz, 2), 4)
+    core = lax.rem(gz, 2)
+    x_on = [lax.rem(place_x + i, 4) * 8 for i in range(4)]
+    y_on = [lax.rem(place_y + i, 4) * 2 for i in range(4)]
+    cores = (core, 1 - core)
+    me = gy * N_GZ + gz
+
+    def onward(own, k):
+        return lax.rem(own + 10 - lax.div(k * (k + 1), 2), 4)
+
     def to_all(src, dst, n):
         dst[:, pl.ds(me, 1), :] = src[:, pl.ds(me, 1), :]
 
-        def one(i, carry):
-            p, peer = peer_of(i)
+        def to_one(column, z):
             pltpu.make_async_remote_copy(
-                src_ref=src.at[:, pl.ds(p, 1)],
+                src_ref=src.at[:, pl.ds(z * N_GZ + column, 1)],
                 dst_ref=dst.at[:, pl.ds(me, 1)],
                 send_sem=all_s.at[n],
                 recv_sem=all_r.at[n],
-                device_id=peer,
+                device_id=(column, z),
                 device_id_type=MESH,
             ).start()
+
+        def to_eight(i, carry):
+            x = onward(place_x, lax.div(i, 4)) * 8
+            z = onward(gy, lax.rem(i, 4))
+            for y in (2, 1, 3, 0):
+                for other in (1, 0):
+                    to_one(x + y_on[y] + cores[other], z)
             return carry
 
-        lax.fori_loop(0, DEVICES - 1, one, 0)
+        lax.fori_loop(0, 15, to_eight, 0)
+        for y in (2, 1, 3, 0):
+            for other in (1, 0):
+                if (y, other) != (0, 0):
+                    to_one(x_on[0] + y_on[y] + cores[other], gy)
         pltpu.make_async_copy(
             src.at[:, pl.ds(0, DEVICES - 1)], dst.at[:, pl.ds(0, DEVICES - 1)], all_r.at[n]
         ).wait()
@@ -569,8 +593,9 @@
     for copy in send_all(thermal, th_moves, th_s, th_r, 0):
         copy.wait()
     pltpu.make_async_copy(
-        ask_send.at[pl.ds(0, DEVICES - 1)], ask_recv.at[pl.ds(0, DEVICES - 1)], all_s.at[0]
+        ask_send.at[: N_GY - 1], ask_mid.at[: N_GY - 1], all_s.at[0]
     ).wait()
+    pltpu.make_async_copy(others, others, all_s.at[3]).wait()
     for n, ref in ((1, row_send), (2, heat_send)):
         done = ref.at[:, pl.ds(0, DEVICES - 1)]
         pltpu.make_async_copy(done, done, all_s.at[n]).wait()
@@ -656,8 +681,9 @@
             pltpu.VMEM((19, DEPTH + 2, PLANE, 128), f32),
             pltpu.VMEM((DEPTH, ROWS, 128), i32),
             pltpu.VMEM((4, DEPTH, ROWS, 128), f32),
-            pltpu.VMEM((DEVICES, 128), f32),
-            pltpu.VMEM((DEVICES, 128), f32),
+            pltpu.VMEM((N_GY, N_GZ, 128), f32),
+            pltpu.VMEM((N_GY, N_GZ, 128), f32),
+            pltpu.VMEM((N_GY, N_GZ, 128), f32),
             pltpu.VMEM((CAP, DEVICES, 128), f32),
             pltpu.VMEM((CAP, DEVICES, 128), f32),
             pltpu.VMEM((CAP, DEVICES, 128), f32),
@@ -674,11 +700,10 @@
             dma((8,)),
             dma((28,)),
             dma((28,)),
-            dma((3,)),
-            dma((3,)),
             dma((4,)),
             dma((4,)),
-            pltpu.SemaphoreType.REGULAR,
+            dma((4,)),
+            dma((4,)),
         ],
         compiler_params=pltpu.CompilerParams(
             collective_id=0, has_side_effects=True, vmem_limit_bytes=40 * 2**20

time: 50.7 us -> 45.7 us (0.901)
  Pallas kernels: 49.9 us -> 44.5 us
    pallas_call x1, Pallas kernels: 48.3 us -> 42.9 us  [per_device(): pl.pallas_call(kernel, out_shape=(pltpu.VMEM((19, CELL_ROWS, 128), f32),...]
where the time goes in v2:
time: 45.7 us; the launch traced here: 45.2 us
  Pallas kernels  44.5 us (97%)
  between operations  0.64 us (1%)
    pallas_call x1, Pallas kernels, per_device(): pl.pallas_call(kernel, out_shape=(pltpu.VMEM((19, CELL_ROWS, 128), f32),...  42.9 us
    pallas_call x1, Pallas kernels, per_device(): pl.pallas_call(finish, out_shape=(jax.ShapeDtypeStruct((19, CELL_ROWS, 12...  1.64 us

profile of v2, /device:TPU:0, one launch (start us, length us, event | category | flops | bytes accessed | tf_op | source)
XLA Modules:
  0.0 45.2 jit_solution(6395653673535014844)
XLA Ops:
  0.6 42.9 %shard_map.95 = (f32[19,288,128]{2,1,0:T(8,128)S(1)}, f32[6,6,88,128]{3,2,1,0:T(8,128)S(1)}, f32[384,128]{1,0:T(8,128)S(1)}) custom-call(f32[19,288,128]{2,1,0:T(8,128)} %bitcast.29, s32[288,128]{1,0:T(8,128)} %bitcast.30, f32[288,128]{1,0:T(8,128)} %bitcast.31, s32[1,64]{1,0:T(1,128)} %line_hbm.1, s32[4,128]{1,0:T(4,128)} %bitcast.33, s32[1,512]{1,0:T(1,128)} %place_hbm.1, ...), custom_call_target="tpu_custom_call" | custom-call | flops 100000000 | bytes 7000000 | tf_op jit(solution)/shard_map/pallas_call | solution.py:661
  43.6 1.6 %shard_map.96 = (f32[19,288,128]{2,1,0:T(8,128)}, f32[288,128]{1,0:T(8,128)}) custom-call(f32[19,288,128]{2,1,0:T(8,128)S(1)} %get-tuple-element.7.field, f32[6,6,88,128]{3,2,1,0:T(8,128)S(1)} %get-tuple-element.8.thermal, f32[384,128]{1,0:T(8,128)S(1)} %get-tuple-element.9.cells), custom_call_target="tpu_custom_call" | custom-call | flops 1000000 | bytes 7000000 | tf_op jit(solution)/shard_map/pallas_call | solution.py:715

commit v3 on v2

--- a/solution.py
+++ b/solution.py
@@ -46,6 +46,7 @@
 PAIRS = [(q, q + 1) for q in range(1, 19, 2)]
 OPP = [0, 2, 1, 4, 3, 6, 5, 8, 7, 10, 9, 12, 11, 14, 13, 16, 15, 18, 17]
 RELAX = 0.8
+THIRDS = (0, 2, 1)
 ORDER = [18, 5, 11, 14, 15, 17, 12, 13, 6, 16, 4, 8, 9, 1, 2, 0, 3, 7, 10]
 SLOT = [ORDER.index(q) for q in range(19)]
 LEFT_BIT = 19
@@ -174,8 +175,8 @@
     return 1 + lax.div(j, 2), lax.rem(j, 2) * 8
 
 
-def face_tile(third):
-    return lambda j: (lax.div(j, 3) * 3, third * 3 + lax.rem(j, 3))
+def face_tile(first_rb, count):
+    return lambda j: (lax.div(j, count) * 3, first_rb + lax.rem(j, count))
 
 
 def any_tile(j):
@@ -244,23 +245,36 @@
     up, down = lax.rem(gz + 1, N_GZ), lax.rem(gz + N_GZ - 1, N_GZ)
     north, south = lax.rem(gy + 1, N_GY), lax.rem(gy + N_GY - 1, N_GY)
 
+    barrier = pltpu.get_barrier_semaphore()
+
+    def greet(i, carry):
+        pl.semaphore_signal(
+            barrier, 1, device_id=(lax.rem(gz + i, N_GZ), gy), device_id_type=MESH
+        )
+        return carry
+
+    lax.fori_loop(1, N_GZ, greet, 0, unroll=N_GZ - 1)
+    for i in range(1, N_GY):
+        pl.semaphore_signal(barrier, 1, device_id=(gz, lax.rem(gy + i, N_GY)), device_id_type=MESH)
+    for peer in ((up, north), (up, south), (down, north), (down, south)):
+        pl.semaphore_signal(barrier, 1, device_id=peer, device_id_type=MESH)
+
     kind_copy = pltpu.make_async_copy(kind_hbm, kind, small_sem.at[6])
     kind_copy.start()
+    want_copy = pltpu.make_async_copy(want_hbm, want, small_sem.at[5])
+    want_copy.start()
 
     def part(rb):
         rows = pl.ds(rb * 32, 32)
         return pltpu.make_async_copy(pop_hbm.at[:, rows], inputs.at[:, rows], load_sem.at[rb])
 
-    def start_part(rb, carry):
-        part(rb).start()
-        return carry
-
-    lax.fori_loop(0, 9, start_part, 0, unroll=9)
+    for third in THIRDS:
+        for rb in range(3 * third, 3 * third + 3):
+            part(rb).start()
 
     small = []
     for i, (src, dst) in enumerate(
         (
-            (want_hbm, want),
             (line_hbm, line),
             (place_hbm, place),
             (hits_hbm, hits),
@@ -272,20 +286,6 @@
         copy.start()
         small.append(copy)
 
-    barrier = pltpu.get_barrier_semaphore()
-
-    def greet(i, carry):
-        pl.semaphore_signal(
-            barrier, 1, device_id=(lax.rem(gz + i, N_GZ), gy), device_id_type=MESH
-        )
-        return carry
-
-    lax.fori_loop(1, N_GZ, greet, 0, unroll=N_GZ - 1)
-    for i in range(1, N_GY):
-        pl.semaphore_signal(barrier, 1, device_id=(gz, lax.rem(gy + i, N_GY)), device_id_type=MESH)
-    for peer in ((up, north), (up, south), (down, north), (down, south)):
-        pl.semaphore_signal(barrier, 1, device_id=peer, device_id_type=MESH)
-
     kind_copy.wait()
 
     def flags(z, rb):
@@ -293,6 +293,17 @@
         gas_pad[z + 1, pl.ds(rb * 8 + PAD, 8), :] = gas.astype(jnp.int32)
 
     over(any_tile, 36, flags, 12)
+
+    want_copy.wait()
+    row, lane = tile_iota(0, (DEVICES, DEVICES)), tile_iota(1, (DEVICES, DEVICES))
+    holder = lane == (row & (N_GZ - 1)) * N_GY + (row >> 5)
+    rows_of = jnp.zeros((DEVICES, DEVICES), jnp.float32)
+    for s in range(CAP):
+        asked = want[s : s + 1, :].astype(jnp.float32)
+        column = jnp.sum(jnp.where(holder, asked, 0.0), axis=1, keepdims=True)
+        rows_of = jnp.where(lane == s, column, rows_of)
+    ask_send[...] = rows_of.reshape(N_GY, N_GZ, DEVICES)
+    ask_mid[gy] = ask_send[gy]
 
     low_src, low_dst = slice(PAD, PAD + 2), slice(PAD + ROWS, PAD + ROWS + 2)
     high_src, high_dst = slice(PAD + ROWS - 2, PAD + ROWS), slice(PAD - 2, PAD)
@@ -311,8 +322,8 @@
         copy.start()
         return copy
 
-    def face_moves(third):
-        rows = slice(PAD + 24 * third, PAD + 24 * third + 24)
+    def face_moves(first_rb, count):
+        rows = slice(PAD + 8 * first_rb, PAD + 8 * (first_rb + count))
         return (
             ((slice(0, 5), 4, rows), (slice(0, 5), 0, rows), (up, gy)),
             ((slice(5, 10), 1, rows), (slice(5, 10), 5, rows), (down, gy)),
@@ -356,42 +367,32 @@
         for i in range(4):
             vel[i, z, pl.ds(rb * 8, 8), :] = velocity[i]
 
-    faces1, gas_copies = [], []
-    for third in range(3):
+    def ask_row():
+        for i in range(1, N_GY):
+            peer = lax.rem(gy + i, N_GY)
+            pltpu.make_async_remote_copy(
+                src_ref=ask_send.at[peer],
+                dst_ref=ask_mid.at[gy],
+                send_sem=all_s.at[0],
+                recv_sem=all_r.at[0],
+                device_id=(gz, peer),
+                device_id_type=MESH,
+            ).start()
+
+    pl.semaphore_wait(barrier, N_GZ - 1 + N_GY - 1 + 4)
+    gas_copies = send_all(gas_pad, gas_moves, gas_s, gas_r, 0)
+    ask_row()
+    faces1 = []
+    for third in THIRDS:
         for rb in range(3 * third, 3 * third + 3):
             part(rb).wait()
         over(lambda j: (lax.div(j, 3), 3 * third + lax.rem(j, 3)), 12, first)
-        if third == 0:
-            pl.semaphore_wait(barrier, N_GZ - 1 + N_GY - 1 + 4)
-        faces1 += send_all(post1, face_moves(third), halo_s, halo_r, 2 * third)
-        if third == 0:
-            gas_copies += send_all(gas_pad, gas_moves[:2], gas_s, gas_r, 0)
-        if third == 1:
-            gas_copies += send_all(gas_pad, gas_moves[2:], gas_s, gas_r, 2)
-    sides1 = send_all(post1, side_moves, halo_s, halo_r, 6)
-    corners1 = send_all(post1, corner_moves, halo_s, halo_r, 10)
-
+        faces1.append(send_all(post1, face_moves(3 * third, 3), halo_s, halo_r, 2 * third))
+        if third == THIRDS[1]:
+            corners1 = send_all(post1, corner_moves, halo_s, halo_r, 10)
+            sides1 = send_all(post1, side_moves, halo_s, halo_r, 6)
     for copy in small:
         copy.wait()
-    row, lane = tile_iota(0, (DEVICES, DEVICES)), tile_iota(1, (DEVICES, DEVICES))
-    holder = lane == (row & (N_GZ - 1)) * N_GY + (row >> 5)
-    rows_of = jnp.zeros((DEVICES, DEVICES), jnp.float32)
-    for s in range(CAP):
-        asked = want[s : s + 1, :].astype(jnp.float32)
-        column = jnp.sum(jnp.where(holder, asked, 0.0), axis=1, keepdims=True)
-        rows_of = jnp.where(lane == s, column, rows_of)
-    ask_send[...] = rows_of.reshape(N_GY, N_GZ, DEVICES)
-    ask_mid[gy] = ask_send[gy]
-    for i in range(1, N_GY):
-        peer = lax.rem(gy + i, N_GY)
-        pltpu.make_async_remote_copy(
-            src_ref=ask_send.at[peer],
-            dst_ref=ask_mid.at[gy],
-            send_sem=all_s.at[0],
-            recv_sem=all_r.at[0],
-            device_id=(gz, peer),
-            device_id_type=MESH,
-        ).start()
 
     def ask_columns():
         pltpu.make_async_copy(
@@ -441,19 +442,40 @@
     for copy in gas_copies:
         copy.wait()
     over(side_tile, 4, masks)
-    for third in range(3):
-        over(face_tile(third), 6, masks)
+    over(face_tile(0, 9), 18, masks, 9)
     for copy in sides1:
         copy.wait()
     over(side_tile, 4, second)
-    for copy in faces1 + corners1:
-        copy.wait()
     faces2 = []
-    for third in range(3):
-        over(face_tile(third), 6, second)
-        faces2 += send_all(post2, face_moves(third), halo_s, halo_r, 14 + 2 * third)
-    corners2 = send_all(post2, corner_moves, halo_s, halo_r, 24)
-    sides2 = send_all(post2, side_moves, halo_s, halo_r, 20)
+
+    def second_faces(first_rb, count):
+        over(face_tile(first_rb, count), 2 * count, second)
+
+    def send_faces(first_rb, count):
+        faces2.append(
+            send_all(post2, face_moves(first_rb, count), halo_s, halo_r, 14 + 2 * len(faces2))
+        )
+
+    for copy in faces1[0]:
+        copy.wait()
+    second_faces(1, 1)
+    for copy in faces1[1]:
+        copy.wait()
+    second_faces(7, 1)
+    for copy in corners1:
+        copy.wait()
+    second_faces(0, 1)
+    send_faces(0, 2)
+    second_faces(8, 1)
+    send_faces(7, 2)
+    corners2 = send_all(post2, corner_moves, halo_s, halo_r, 26)
+    sides2 = send_all(post2, side_moves, halo_s, halo_r, 22)
+    for copy in faces1[2]:
+        copy.wait()
+    second_faces(2, 3)
+    send_faces(2, 3)
+    second_faces(5, 2)
+    send_faces(5, 2)
 
     big0, big1 = tile_iota(0, (SLOTS, SLOTS)), tile_iota(1, (SLOTS, SLOTS))
     diagonal = big0 == big1
@@ -512,10 +534,16 @@
     for copy in sides2:
         copy.wait()
     over(side_tile, 4, last)
-    for copy in faces2 + corners2:
-        copy.wait()
-    for third in range(3):
-        over(face_tile(third), 6, last)
+    for copy in faces2[0] + faces2[1] + corners2:
+        copy.wait()
+    over(face_tile(0, 1), 2, last)
+    over(face_tile(8, 1), 2, last)
+    for copy in faces2[2]:
+        copy.wait()
+    over(face_tile(1, 3), 6, last)
+    for copy in faces2[3]:
+        copy.wait()
+    over(face_tile(4, 4), 8, last)
 
     place_x, place_y = lax.div(gz, 8), lax.rem(lax.div(gz, 2), 4)
     core = lax.rem(gz, 2)
@@ -583,7 +611,7 @@
             thermal[2 * i + 1, z + 1, pl.ds(rb * 8 + PAD, 8), :] = eighth - moved
         cells[at, :] = 0.25 * source
 
-    over(any_tile, 36, sources, 12)
+    over(any_tile, 36, sources)
     th_moves = (
         ((4, 4, body), (4, 0, body), (up, gy)),
         ((5, 1, body), (5, 5, body), (down, gy)),
@@ -698,8 +726,8 @@
             dma((7,)),
             dma((8,)),
             dma((8,)),
-            dma((28,)),
-            dma((28,)),
+            dma((30,)),
+            dma((30,)),
             dma((4,)),
             dma((4,)),
             dma((4,)),

time: 45.7 us -> 43.6 us (0.954)
  Pallas kernels: 44.5 us -> 42.5 us
    pallas_call x1, Pallas kernels: 42.9 us -> 40.8 us  [per_device(): pl.pallas_call(kernel, out_shape=(pltpu.VMEM((19, CELL_ROWS, 128), f32),...]
where the time goes in v3:
time: 43.6 us; the launch traced here: 43.1 us
  Pallas kernels  42.5 us (97%)
  between operations  0.64 us (1%)
    pallas_call x1, Pallas kernels, per_device(): pl.pallas_call(kernel, out_shape=(pltpu.VMEM((19, CELL_ROWS, 128), f32),...  40.8 us
    pallas_call x1, Pallas kernels, per_device(): pl.pallas_call(finish, out_shape=(jax.ShapeDtypeStruct((19, CELL_ROWS, 12...  1.64 us

profile of v3, /device:TPU:0, one launch (start us, length us, event | category | flops | bytes accessed | tf_op | source)
XLA Modules:
  0.0 43.1 jit_solution(13112896423353729674)
XLA Ops:
  0.6 40.8 %shard_map.95 = (f32[19,288,128]{2,1,0:T(8,128)S(1)}, f32[6,6,88,128]{3,2,1,0:T(8,128)S(1)}, f32[384,128]{1,0:T(8,128)S(1)}) custom-call(f32[19,288,128]{2,1,0:T(8,128)} %bitcast.29, s32[288,128]{1,0:T(8,128)} %bitcast.30, f32[288,128]{1,0:T(8,128)} %bitcast.31, s32[1,64]{1,0:T(1,128)} %line_hbm.1, s32[4,128]{1,0:T(4,128)} %bitcast.33, s32[1,512]{1,0:T(1,128)} %place_hbm.1, ...), custom_call_target="tpu_custom_call" | custom-call | flops 100000000 | bytes 7000000 | tf_op jit(solution)/shard_map/pallas_call | solution.py:689
  41.5 1.6 %shard_map.96 = (f32[19,288,128]{2,1,0:T(8,128)}, f32[288,128]{1,0:T(8,128)}) custom-call(f32[19,288,128]{2,1,0:T(8,128)S(1)} %get-tuple-element.7.field, f32[6,6,88,128]{3,2,1,0:T(8,128)S(1)} %get-tuple-element.8.thermal, f32[384,128]{1,0:T(8,128)S(1)} %get-tuple-element.9.cells), custom_call_target="tpu_custom_call" | custom-call | flops 1000000 | bytes 7000000 | tf_op jit(solution)/shard_map/pallas_call | solution.py:743

commit v4 on v3

--- a/solution.py
+++ b/solution.py
@@ -552,8 +552,18 @@
     cores = (core, 1 - core)
     me = gy * N_GZ + gz
 
-    def onward(own, k):
-        return lax.rem(own + 10 - lax.div(k * (k + 1), 2), 4)
+    z_on = [lax.rem(gy + i, N_GY) for i in range(4)]
+
+    def chips(partner):
+        return sum(min(step, 4 - step) for step in partner[:3])
+
+    partners = [
+        ((7 * i) % 4, (i // 4 + i) % 4, (i // 16 + i // 4) % 4, other)
+        for i in range(64)
+        for other in (1, 0)
+    ]
+    partners = sorted(set(partners) - {(0, 0, 0, 0)}, key=lambda p: (-chips(p), partners.index(p)))
+    assert len(partners) == DEVICES - 1
 
     def to_all(src, dst, n):
         dst[:, pl.ds(me, 1), :] = src[:, pl.ds(me, 1), :]
@@ -568,19 +578,8 @@
                 device_id_type=MESH,
             ).start()
 
-        def to_eight(i, carry):
-            x = onward(place_x, lax.div(i, 4)) * 8
-            z = onward(gy, lax.rem(i, 4))
-            for y in (2, 1, 3, 0):
-                for other in (1, 0):
-                    to_one(x + y_on[y] + cores[other], z)
-            return carry
-
-        lax.fori_loop(0, 15, to_eight, 0)
-        for y in (2, 1, 3, 0):
-            for other in (1, 0):
-                if (y, other) != (0, 0):
-                    to_one(x_on[0] + y_on[y] + cores[other], gy)
+        for x, y, z, other in partners:
+            to_one(x_on[x] + y_on[y] + cores[other], z_on[z])
         pltpu.make_async_copy(
             src.at[:, pl.ds(0, DEVICES - 1)], dst.at[:, pl.ds(0, DEVICES - 1)], all_r.at[n]
         ).wait()

time: 43.6 us -> 42.7 us (0.979)
  Pallas kernels: 42.5 us -> 41.9 us
    pallas_call x1, Pallas kernels: 40.8 us -> 40.2 us  [per_device(): pl.pallas_call(kernel, out_shape=(pltpu.VMEM((19, CELL_ROWS, 128), f32),...]
where the time goes in v4:
time: 42.7 us; the launch traced here: 42.5 us
  Pallas kernels  41.9 us (98%)
  between operations  0.64 us (1%)
    pallas_call x1, Pallas kernels, per_device(): pl.pallas_call(kernel, out_shape=(pltpu.VMEM((19, CELL_ROWS, 128), f32),...  40.2 us
    pallas_call x1, Pallas kernels, per_device(): pl.pallas_call(finish, out_shape=(jax.ShapeDtypeStruct((19, CELL_ROWS, 12...  1.64 us

profile of v4, /device:TPU:0, one launch (start us, length us, event | category | flops | bytes accessed | tf_op | source)
XLA Modules:
  0.0 42.5 jit_solution(7921297669575649416)
XLA Ops:
  0.6 40.2 %shard_map.95 = (f32[19,288,128]{2,1,0:T(8,128)S(1)}, f32[6,6,88,128]{3,2,1,0:T(8,128)S(1)}, f32[384,128]{1,0:T(8,128)S(1)}) custom-call(f32[19,288,128]{2,1,0:T(8,128)} %bitcast.29, s32[288,128]{1,0:T(8,128)} %bitcast.30, f32[288,128]{1,0:T(8,128)} %bitcast.31, s32[1,64]{1,0:T(1,128)} %line_hbm.1, s32[4,128]{1,0:T(4,128)} %bitcast.33, s32[1,512]{1,0:T(1,128)} %place_hbm.1, ...), custom_call_target="tpu_custom_call" | custom-call | flops 100000000 | bytes 7000000 | tf_op jit(solution)/shard_map/pallas_call | solution.py:688
  40.9 1.6 %shard_map.96 = (f32[19,288,128]{2,1,0:T(8,128)}, f32[288,128]{1,0:T(8,128)}) custom-call(f32[19,288,128]{2,1,0:T(8,128)S(1)} %get-tuple-element.7.field, f32[6,6,88,128]{3,2,1,0:T(8,128)S(1)} %get-tuple-element.8.thermal, f32[384,128]{1,0:T(8,128)S(1)} %get-tuple-element.9.cells), custom_call_target="tpu_custom_call" | custom-call | flops 1000000 | bytes 7000000 | tf_op jit(solution)/shard_map/pallas_call | solution.py:742

commit v5 on v4

--- a/solution.py
+++ b/solution.py
@@ -566,7 +566,6 @@
     assert len(partners) == DEVICES - 1
 
     def to_all(src, dst, n):
-        dst[:, pl.ds(me, 1), :] = src[:, pl.ds(me, 1), :]
 
         def to_one(column, z):
             pltpu.make_async_remote_copy(
@@ -580,6 +579,7 @@
 
         for x, y, z, other in partners:
             to_one(x_on[x] + y_on[y] + cores[other], z_on[z])
+        dst[:, pl.ds(me, 1), :] = src[:, pl.ds(me, 1), :]
         pltpu.make_async_copy(
             src.at[:, pl.ds(0, DEVICES - 1)], dst.at[:, pl.ds(0, DEVICES - 1)], all_r.at[n]
         ).wait()
@@ -610,14 +610,18 @@
             thermal[2 * i + 1, z + 1, pl.ds(rb * 8 + PAD, 8), :] = eighth - moved
         cells[at, :] = 0.25 * source
 
-    over(any_tile, 36, sources)
     th_moves = (
         ((4, 4, body), (4, 0, body), (up, gy)),
         ((5, 1, body), (5, 5, body), (down, gy)),
         ((2, planes, high_src), (2, planes, high_dst), (gz, north)),
         ((3, planes, low_src), (3, planes, low_dst), (gz, south)),
     )
-    for copy in send_all(thermal, th_moves, th_s, th_r, 0):
+    over(face_tile(0, 9), 18, sources)
+    th_copies = send_all(thermal, th_moves[:2], th_s, th_r, 0)
+    over(side_tile, 4, sources)
+    th_copies += send_all(thermal, th_moves[2:], th_s, th_r, 2)
+    over(inner_tile, 14, sources)
+    for copy in th_copies:
         copy.wait()
     pltpu.make_async_copy(
         ask_send.at[: N_GY - 1], ask_mid.at[: N_GY - 1], all_s.at[0]

time: 42.7 us -> 42.7 us (level)
  no operation moved by 1% of the time
where the time goes in v5:
time: 42.7 us; the launch traced here: 42.5 us
  Pallas kernels  41.8 us (98%)
  between operations  0.64 us (1%)
    pallas_call x1, Pallas kernels, per_device(): pl.pallas_call(kernel, out_shape=(pltpu.VMEM((19, CELL_ROWS, 128), f32),...  40.2 us
    pallas_call x1, Pallas kernels, per_device(): pl.pallas_call(finish, out_shape=(jax.ShapeDtypeStruct((19, CELL_ROWS, 12...  1.64 us

profile of v5, /device:TPU:0, one launch (start us, length us, event | category | flops | bytes accessed | tf_op | source)
XLA Modules:
  0.0 42.5 jit_solution(16262600615288401476)
XLA Ops:
  0.6 40.2 %shard_map.95 = (f32[19,288,128]{2,1,0:T(8,128)S(1)}, f32[6,6,88,128]{3,2,1,0:T(8,128)S(1)}, f32[384,128]{1,0:T(8,128)S(1)}) custom-call(f32[19,288,128]{2,1,0:T(8,128)} %bitcast.29, s32[288,128]{1,0:T(8,128)} %bitcast.30, f32[288,128]{1,0:T(8,128)} %bitcast.31, s32[1,64]{1,0:T(1,128)} %line_hbm.1, s32[4,128]{1,0:T(4,128)} %bitcast.33, s32[1,512]{1,0:T(1,128)} %place_hbm.1, ...), custom_call_target="tpu_custom_call" | custom-call | flops 100000000 | bytes 7000000 | tf_op jit(solution)/shard_map/pallas_call | solution.py:692
  40.9 1.6 %shard_map.96 = (f32[19,288,128]{2,1,0:T(8,128)}, f32[288,128]{1,0:T(8,128)}) custom-call(f32[19,288,128]{2,1,0:T(8,128)S(1)} %get-tuple-element.7.field, f32[6,6,88,128]{3,2,1,0:T(8,128)S(1)} %get-tuple-element.8.thermal, f32[384,128]{1,0:T(8,128)S(1)} %get-tuple-element.9.cells), custom_call_target="tpu_custom_call" | custom-call | flops 1000000 | bytes 7000000 | tf_op jit(solution)/shard_map/pallas_call | solution.py:746
